TPU v7x, 128 devices: a whole 4x4x4 slice. The times are simulated.
128 devices in a mesh: ix: 4 (over z), iy: 4 (over x), depth: 8 (over y, core).
Axes of the slice: x: 4, y: 4, z: 4, core: 2. Of those that a mesh axis runs over, the one named last changes fastest.
Arguments:
- density: bfloat16 [512, 1024, 1024], P('depth', 'ix', 'iy'), may hold values from -4 to 4
Outputs:
- image: float32 [4, 1024, 1024], P(None, ('ix', 'depth'), 'iy')
All inputs are finite; a program needn't handle non-finite values.
Results may differ from a plain program's by a relative error of at most 0.0003.
Values may be sent and summed in bfloat16 or wider, within the bound.
A program may use at most 128 MiB of HBM per device.

v0:
```python
import jax
import jax.numpy as jnp
from jax import lax
from jax.sharding import PartitionSpec as P


def extended(cells, sides, width):
    for axis, dim in sides:
        count = lax.axis_size(axis)
        ends = count - 1
        head = lax.slice_in_dim(cells, 0, width, axis=dim)
        tail = lax.slice_in_dim(cells, cells.shape[dim] - width, cells.shape[dim], axis=dim)
        cells = jnp.concatenate(
            [
                lax.ppermute(tail, axis, [(i, (i + 1) % count) for i in range(ends)]),
                cells,
                lax.ppermute(head, axis, [((i + 1) % count, i) for i in range(ends)]),
            ],
            axis=dim,
        )
    return cells


def prefix(part, axis, combine, identity):
    place = lax.axis_index(axis)
    gathered = lax.all_gather(part, axis)
    state = jnp.zeros_like(part) + jnp.asarray(identity, part.dtype)

    def one(turn, state):
        return combine(state, lax.dynamic_index_in_dim(gathered, turn, 0, False))

    return lax.fori_loop(0, place, one, state)


def offset_view(volume, shift_z, shift_x, shift_y):
    size_z = volume.shape[0] - 4
    size_x = volume.shape[1] - 4
    size_y = volume.shape[2] - 4
    return volume[
        2 + shift_z : 2 + shift_z + size_z,
        2 + shift_x : 2 + shift_x + size_x,
        2 + shift_y : 2 + shift_y + size_y,
    ]


def derivative(volume, direction_unit):
    samples = [offset_view(volume, *[k * u for u in direction_unit]) for k in (2, 1, -1, -2)]
    return (8.0 * (samples[1] - samples[2]) - (samples[0] - samples[3])) / 12.0


def shade_brick(volume, spacing):
    center = offset_view(volume, 0, 0, 0)
    slope_z = derivative(volume, (1, 0, 0))
    slope_x = derivative(volume, (0, 1, 0))
    slope_y = derivative(volume, (0, 0, 1))
    facing = jnp.abs(0.48 * slope_z + 0.6 * slope_x + 0.64 * slope_y) * lax.rsqrt(
        slope_z * slope_z + slope_x * slope_x + slope_y * slope_y + 1.0
    )
    brightness = 0.3 + 0.7 * facing
    extinct = 0.2 * jnp.cosh(2.0 * center)
    cell_alpha = 1.0 - jnp.exp(-spacing * extinct)
    optical_before = jnp.cumsum(extinct, axis=0) - extinct
    weights = jnp.exp(-spacing * optical_before) * cell_alpha * brightness
    channel_red = jnp.sum(weights * jax.nn.sigmoid(2.0 * center), axis=0)
    channel_green = jnp.sum(weights * jnp.exp(-center * center), axis=0)
    channel_blue = jnp.sum(weights * jax.nn.sigmoid(-2.0 * center), axis=0)
    optical_depth = spacing * jnp.sum(extinct, axis=0)
    return (channel_red, channel_green, channel_blue, optical_depth)


def add_terms(earlier, later):
    return earlier + later


def on_device(density):
    padded = extended(density, (("depth", 0), ("ix", 1), ("iy", 2)), 2)
    depth_cells = density.shape[0] * lax.axis_size("depth")
    spacing = 1.0 / depth_cells
    channel_red, channel_green, channel_blue, optical_depth = shade_brick(
        padded.astype(jnp.float32), spacing
    )
    optical_front = prefix(optical_depth, "depth", add_terms, jnp.zeros_like(optical_depth))
    transmit = jnp.exp(-optical_front)
    layers = jnp.stack(
        [
            transmit * channel_red,
            transmit * channel_green,
            transmit * channel_blue,
            transmit * (1.0 - jnp.exp(-optical_depth)),
        ]
    )
    image = lax.psum_scatter(layers, "depth", scatter_dimension=1, tiled=True)
    return image


def solution(mesh):
    placed = (P("depth", "ix", "iy"),)
    return jax.shard_map(
        on_device,
        mesh=mesh,
        in_specs=placed,
        out_specs=P(None, ("ix", "depth"), "iy"),
        check_vma=False,
    )
```

profile of v0, /device:TPU:1, one launch (start us, length us, event | category | flops | bytes accessed | tf_op | source)
XLA Modules:
  0.0 414.1 jit_solution(15090249373793358547)
XLA Ops:
  6.5 1.1 fusion.17
  7.6 4.6 %collective-permute-start = (bf16[2,256,256]{2,1,0:T(8,128)(2,1)S(1)}, bf16[2,256,256]{2,1,0:T(8,128)(2,1)S(1)}, u32[]{:S(2)}, u32[]{:S(2)}) collective-permute-start(bf16[2,256,256]{2,1,0:T(8,128)(2,1)S(1)} %get-tuple-element.46), channel_id=1, source_target_pairs={{0,1},{1,2},{2,3},{3,4},{4,5},{5,6},{6,7},{8,9},{9,10},{10,11},{11... | collective-permute-start | bytes 786440 | tf_op jit(solution)/shard_map/ppermute | solution.py:15
  12.2 1.9 collective-permute-start.1
  14.1 1.4 collective-permute-done
  16.2 7.6 %constant_dynamic-update-slice_fusion.1 = bf16[68,256,256]{2,1,0:T(8,128)(2,1)} fusion(bf16[68,256,256]{2,1,0:T(8,128)(2,1)} %constant_dynamic-update-slice_fusion.2, bf16[64,256,256]{2,1,0:T(8,128)(2,1)} %param.3), kind=kLoop, calls=%fused_computation.35 | loop fusion | bytes 16777216
  24.6 1.2 fusion.16
  25.7 3.5 collective-permute-start.2
  29.3 1.3 collective-permute-start.3
  30.6 3.9 collective-permute-done.3
  34.5 6.3 %pad_maximum_fusion = bf16[68,260,256]{2,1,0:T(8,128)(2,1)S(1)} fusion(bf16[68,2,256]{2,1,0:T(2,128)(2,1)S(1)} %collective-permute-done.3, bf16[68,256,256]{2,1,0:T(8,128)(2,1)} %constant_dynamic-update-slice_fusion, bf16[68,2,256]{2,1,0:T(2,128)(2,1)S(1)} %collective-permute-done.2), kind=kLoop, calls=%fused_computation.25 | loop fusion | flops 27156480 | bytes 18104320 | tf_op jit(solution)/shard_map/concatenate | solution.py:13
  40.8 5.5 %fusion.15 = (bf16[68,260,2]{2,1,0:T(8,128)(2,1)}, bf16[68,260,2]{2,1,0:T(8,128)(2,1)}) fusion(bf16[68,260,256]{2,1,0:T(8,128)(2,1)S(1)} %pad_maximum_fusion), kind=kLoop, calls=%fused_computation.40 | loop fusion | bytes 282880 | tf_op jit(solution)/shard_map/slice | solution.py:12
  46.4 4.4 %copy.2 = bf16[68,260,2]{1,2,0:T(2,128)(2,1)S(1)} copy(bf16[68,260,2]{2,1,0:T(8,128)(2,1)} %get-tuple-element.41) | data formatting | bytes 141440 | tf_op jit(solution)/shard_map/slice | solution.py:12
  50.8 3.1 collective-permute-start.4
  53.9 4.4 %copy.3 = bf16[68,260,2]{1,2,0:T(2,128)(2,1)S(1)} copy(bf16[68,260,2]{2,1,0:T(8,128)(2,1)} %get-tuple-element.42) | data formatting | bytes 141440 | tf_op jit(solution)/shard_map/slice | solution.py:11
  58.3 1.5 collective-permute-start.5
  59.8 3.5 copy.4
  63.7 3.6 copy.5
  67.3 21.8 %maximum_convert_fusion = f32[68,260,260]{2,1,0:T(8,128)} fusion(bf16[68,260,2]{2,1,0:T(8,128)(2,1)} %copy.5, bf16[68,2,256]{2,1,0:T(2,128)(2,1)S(1)} %collective-permute-done.3, bf16[68,256,256]{2,1,0:T(8,128)(2,1)} %constant_dynamic-update-slice_fusion, bf16[68,2,256]{2,1,0:T(2,128)(2,1)S(1)} %collective-permute-done.2, bf16[68,260,2]{2,1,0:T(8,128)(2,1)} %copy.4), kind=kLoop, calls=%fused_computation.24 | loop fusion | flops 45968000 | bytes 27580800 | tf_op jit(solution)/shard_map/convert_element_type | solution.py:80
  89.1 249.5 %multiply_reduce_fusion.1 = (f32[256,256]{1,0:T(8,128)S(1)}, f32[256,256]{1,0:T(8,128)S(1)}, f32[256,256]{1,0:T(8,128)S(1)}, f32[256,256]{1,0:T(8,128)S(1)}) fusion(f32[68,260,260]{2,1,0:T(8,128)} %maximum_convert_fusion), kind=kOutput, calls=%fused_computation.18 | output fusion | flops 524025856 | bytes 235929600 | tf_op jit(solution)/shard_map/jit(cumsum)/reduce_window_sum | solution.py:62
  339.5 30.6 %all-gather.3.cloned.1.call-done = f32[2048,256]{1,0:T(8,128)} async-done(((f32[256,256]{1,0:T(8,128)}), f32[2048,256]{1,0:T(8,128)}) %all-gather.3.cloned.1.call-update) | async-done | bytes 2097168 | tf_op jit(solution)/shard_map/all_gather | solution.py:26
  370.1 1.0 while.10
  370.2 1.0 bitcast_add_fusion.2
  371.3 1.1 pad_maximum_fusion.1
  372.4 34.9 %reduce-scatter.2.cloned.1.call-done = f32[4,32,256]{2,1,0:T(8,128)} async-done(((f32[4,256,256]{2,1,0:T(8,128)}), f32[4,32,256]{2,1,0:T(8,128)}) %reduce-scatter.2.cloned.1.call-update) | async-done | bytes 131088 | tf_op jit(solution)/shard_map/reduce_scatter | solution.py:92
  (13 shorter events, 2.8 us)
Async XLA Ops:
  6.5 363.6 %all-gather.3.cloned.1.call-start = ((), (), s32[]{:S(2)}) async-start(), calls=%async_computation.2 | async-start | bytes 2359296 | tf_op jit(solution)/shard_map/all_gather | solution.py:26
  7.6 7.9 %collective-permute-start = (bf16[2,256,256]{2,1,0:T(8,128)(2,1)S(1)}, bf16[2,256,256]{2,1,0:T(8,128)(2,1)S(1)}, u32[]{:S(2)}, u32[]{:S(2)}) collective-permute-start(bf16[2,256,256]{2,1,0:T(8,128)(2,1)S(1)} %get-tuple-element.46), channel_id=1, source_target_pairs={{0,1},{1,2},{2,3},{3,4},{4,5},{5,6},{6,7},{8,9},{9,10},{10,11},{11... | collective-permute-start | bytes 786440 | tf_op jit(solution)/shard_map/ppermute | solution.py:15
  12.2 11.7 %collective-permute-start.1 = (bf16[2,256,256]{2,1,0:T(8,128)(2,1)S(1)}, bf16[2,256,256]{2,1,0:T(8,128)(2,1)S(1)}, u32[]{:S(2)}, u32[]{:S(2)}) collective-permute-start(bf16[2,256,256]{2,1,0:T(8,128)(2,1)S(1)} %get-tuple-element.45), channel_id=1, source_target_pairs={{1,0},{2,1},{3,2},{4,3},{5,4},{6,5},{7,6},{9,8},{10,9},{11,10},{12... | collective-permute-start | bytes 786440 | tf_op jit(solution)/shard_map/ppermute | solution.py:17
  25.7 4.9 %collective-permute-start.2 = (bf16[68,2,256]{2,1,0:T(2,128)(2,1)S(1)}, bf16[68,2,256]{2,1,0:T(2,128)(2,1)S(1)}, u32[]{:S(2)}, u32[]{:S(2)}) collective-permute-start(bf16[68,2,256]{2,1,0:T(2,128)(2,1)S(1)} %get-tuple-element.43), channel_id=1, source_target_pairs={{0,32},{32,64},{64,96},{1,33},{33,65},{65,97},{2,34},{34,66},{66,9... | collective-permute-start | bytes 208904 | tf_op jit(solution)/shard_map/ppermute | solution.py:15
  29.3 5.2 %collective-permute-start.3 = (bf16[68,2,256]{2,1,0:T(2,128)(2,1)S(1)}, bf16[68,2,256]{2,1,0:T(2,128)(2,1)S(1)}, u32[]{:S(2)}, u32[]{:S(2)}) collective-permute-start(bf16[68,2,256]{2,1,0:T(2,128)(2,1)S(1)} %get-tuple-element.44), channel_id=1, source_target_pairs={{32,0},{64,32},{96,64},{33,1},{65,33},{97,65},{34,2},{66,34},{98,6... | collective-permute-start | bytes 208904 | tf_op jit(solution)/shard_map/ppermute | solution.py:17
  50.8 9.0 %collective-permute-start.4 = (bf16[68,260,2]{1,2,0:T(2,128)(2,1)S(1)}, bf16[68,260,2]{1,2,0:T(2,128)(2,1)S(1)}, u32[]{:S(2)}, u32[]{:S(2)}) collective-permute-start(bf16[68,260,2]{1,2,0:T(2,128)(2,1)S(1)} %copy.2), channel_id=1, source_target_pairs={{0,8},{8,16},{16,24},{1,9},{9,17},{17,25},{2,10},{10,18},{18,26},{... | collective-permute-start | bytes 212168 | tf_op jit(solution)/shard_map/ppermute | solution.py:15
  58.3 5.4 %collective-permute-start.5 = (bf16[68,260,2]{1,2,0:T(2,128)(2,1)S(1)}, bf16[68,260,2]{1,2,0:T(2,128)(2,1)S(1)}, u32[]{:S(2)}, u32[]{:S(2)}) collective-permute-start(bf16[68,260,2]{1,2,0:T(2,128)(2,1)S(1)} %copy.3), channel_id=1, source_target_pairs={{8,0},{16,8},{24,16},{9,1},{17,9},{25,17},{10,2},{18,10},{26,18},{... | collective-permute-start | bytes 212168 | tf_op jit(solution)/shard_map/ppermute | solution.py:17
  339.4 67.9 %reduce-scatter.2.cloned.1.call-start = ((), (), s32[]{:S(2)}) async-start(), calls=%async_computation.1 | async-start | bytes 1179648 | tf_op jit(solution)/shard_map/reduce_scatter | solution.py:92
Sparse Core Ops, SparseCore 0:
  339.6 30.5 all-gather.2
  372.5 34.7 reduce-scatter.1
where the time goes:
time: 417 us; the launch traced here: 414 us
  other arithmetic  281 us (67%)
  waiting for transfers between devices  71.3 us (17%)
  local copies, waits for them, and re-layouts  32.7 us (8%)
  starting transfers between devices  16 us (4%)
  between operations  13.5 us (3%)
    another operation x1, other arithmetic, shade_brick(): optical_before = jnp.cumsum(extinct, axis=0) - extinct  250 us
    reduce_scatter x1, waiting for transfers between devices, on_device(): image = lax.psum_scatter(layers, 'depth', scatter_dimension=1, tiled=True)  34.9 us
    all_gather x1, waiting for transfers between devices, prefix(): gathered = lax.all_gather(part, axis)  30.6 us
    convert_element_type x1, other arithmetic, on_device(): padded.astype(jnp.float32)  21.8 us
    ppermute x3, starting transfers between devices, extended(): lax.ppermute(tail, axis, [(i, (i + 1) % count) for i in range(ends)])  11.3 us
    slice x3, local copies, waits for them, and re-layouts, extended(): lax.slice_in_dim(cells, cells.shape[dim] - width, cells.shape[dim], axis=...  11.1 us
    unnamed x2, local copies, waits for them, and re-layouts  8.35 us
  transfers between devices with their start and end apart: 8, of which 5 were waited for; matrix products, arithmetic and copies ran while one was open for 4% of the time, Pallas kernels for 0%

commit v1 on v0

v1 whole, which is shorter than its diff:
```python
import jax
import jax.numpy as jnp
import numpy as np
from jax import lax
from jax.experimental import pallas as pl
from jax.experimental.pallas import tpu as pltpu
from jax.sharding import PartitionSpec as P

MESH = pl.DeviceIdType.MESH
F32, BF16 = jnp.float32, jnp.bfloat16
Z, X, Y = 64, 256, 256
DEPTH = 8
ROWS = X // DEPTH
EDGE = 16
NZ = 512
EXP2_2D = float(2.0 * np.log2(np.e))
EXP2_K = float(-0.1 * np.log2(np.e) / NZ)
EXP2_SQ = float(-np.log2(np.e))
BASE = 25.0 * 0.3 / 0.7
TAPS = ((1, 8.0), (-1, -8.0), (2, -1.0), (-2, 1.0))


def along_y():
    inner = np.zeros((Y, Y), np.float32)
    outer = np.zeros((256, Y), np.float32)
    for y in range(Y):
        for step, tap in TAPS:
            at = y + step
            if 0 <= at < Y:
                inner[at, y] = tap
            elif at < 0:
                outer[[2 * z + at + 2 for z in range(Z)], y] = tap
            else:
                outer[[128 + 2 * z + at - Y for z in range(Z)], y] = tap
    return np.concatenate([inner, outer])


def along_zx():
    start = (0, 32, 64 + 16, 128 + 16, 192, 224)
    out = np.zeros((3, 2, ROWS, 256), np.float32)
    for layer in range(2):
        for row in range(ROWS):
            for step, tap in TAPS:
                across = start[layer + 2] + row + step
                behind = start[layer + 2 + step] + row
                out[0, layer, row, across] += tap
                out[1, layer, row, behind] += tap
                out[2, layer, row, across] += 15 * tap
                out[2, layer, row, behind] += 12 * tap
    return out.reshape(6 * ROWS, 256)


def pick_columns():
    out = np.zeros((Y, 256), np.float32)
    for lane in range(256):
        out[(0 if lane < 128 else Y - 2) + lane % 2, lane] = 1
    return out


def pick_rows():
    out = np.zeros((2, 16, 128), np.float32)
    for layer in range(8):
        for row in range(2):
            out[0, 2 * layer + row, 16 * layer + row] = 1
            out[1, 2 * layer + row, 16 * layer + 14 + row] = 1
    return out


def kernel(
    x_ref, y_mat, zx_mat, col_mat, row_mat, unrow_mat, out_ref,
    cells, halo, pack, row_pack, row_halo, parts, got, gy0, g0, gy1, g1,
    load_sem, z_send, z_recv, x_send, x_recv, y_send, y_recv, send_sem, recv_sem,
):
    me = lax.axis_index("depth")
    ix, iy = lax.axis_index("ix"), lax.axis_index("iy")
    n_ix, n_iy = lax.axis_size("ix"), lax.axis_size("iy")
    front, back = me > 0, me < DEPTH - 1
    up, down = ix > 0, ix < n_ix - 1
    left, right = iy > 0, iy < n_iy - 1

    def load(b):
        rows = pl.ds(pl.multiple_of(ROWS * b, ROWS), ROWS)
        inner = pl.ds(pl.multiple_of(EDGE + ROWS * b, EDGE), ROWS)
        return pltpu.make_async_copy(x_ref.at[:, rows], cells.at[pl.ds(2, Z), inner], load_sem.at[b])

    for b in range(DEPTH):
        load(b).start()

    barrier = pltpu.get_barrier_semaphore()
    for step in range(1, DEPTH):
        pl.semaphore_signal(barrier, inc=1, device_id={"depth": lax.rem(me + step, DEPTH)}, device_id_type=MESH)
    for axis, at, count in (("ix", ix, n_ix), ("iy", iy, n_iy)):
        for step in (1, count - 1):
            pl.semaphore_signal(barrier, inc=1, device_id={axis: lax.rem(at + step, count)}, device_id_type=MESH)
    pl.semaphore_wait(barrier, DEPTH - 1 + 4)

    def remote(src, dst, sems, recvs, k, axis, to):
        return pltpu.make_async_remote_copy(
            src_ref=src, dst_ref=dst, send_sem=sems.at[k], recv_sem=recvs.at[k],
            device_id={axis: to}, device_id_type=MESH,
        )

    body = pl.ds(EDGE, X)
    z_up = remote(x_ref.at[pl.ds(Z - 2, 2)], cells.at[pl.ds(0, 2), body], z_send, z_recv, 0, "depth", lax.rem(me + 1, DEPTH))
    z_dn = remote(x_ref.at[pl.ds(0, 2)], cells.at[pl.ds(Z + 2, 2), body], z_send, z_recv, 1, "depth", lax.rem(me + DEPTH - 1, DEPTH))
    x_up = remote(row_pack.at[1], row_halo.at[0], x_send, x_recv, 0, "ix", lax.rem(ix + 1, n_ix))
    x_dn = remote(row_pack.at[0], row_halo.at[1], x_send, x_recv, 1, "ix", lax.rem(ix + n_ix - 1, n_ix))
    y_up = remote(pack.at[1], halo.at[0], y_send, y_recv, 0, "iy", lax.rem(iy + 1, n_iy))
    y_dn = remote(pack.at[0], halo.at[1], y_send, y_recv, 1, "iy", lax.rem(iy + n_iy - 1, n_iy))

    pl.when(back)(z_up.start)
    pl.when(front)(z_dn.start)

    @pl.when(jnp.logical_not(front))
    def _():
        cells[0:2] = jnp.zeros((2,) + cells.shape[1:], BF16)

    @pl.when(jnp.logical_not(back))
    def _():
        cells[Z + 2 : Z + 4] = jnp.zeros((2,) + cells.shape[1:], BF16)

    for b in range(DEPTH):
        load(b).wait()

    def pack_rows(c, _):
        layers = pl.ds(2 + 8 * c, 8)
        at = pl.ds(pl.multiple_of(16 * c, 16), 16)
        for side, row in ((0, EDGE), (1, X)):
            tiles = cells[layers, row : row + 16].reshape(128, Y)
            row_pack[side, at] = jnp.dot(row_mat[side], tiles, preferred_element_type=F32).astype(BF16)
        return 0

    lax.fori_loop(0, Z // 8, pack_rows, 0)
    pl.when(down)(x_up.start)
    pl.when(up)(x_dn.start)

    def pack_columns(b, _):
        rows = pl.ds(pl.multiple_of(EDGE + ROWS * b, EDGE), ROWS)
        layer_of = (lax.broadcasted_iota(jnp.int32, (ROWS, 256), 1) & 127) >> 1

        def chunk(c, total):
            tiles = cells[pl.ds(2 + 8 * c, 8), rows].reshape(8 * ROWS, Y)
            picked = jnp.dot(tiles, col_mat[...], preferred_element_type=F32).reshape(8, ROWS, 256)
            for i in range(8):
                total = jnp.where(layer_of == 8 * c + i, picked[i], total)
            return total

        total = lax.fori_loop(0, Z // 8, chunk, jnp.zeros((ROWS, 256), F32)).astype(BF16)
        at = pl.ds(pl.multiple_of(ROWS * b, ROWS), ROWS)
        pack[0, at] = total[:, :128]
        pack[1, at] = total[:, 128:]
        return 0

    lax.fori_loop(0, DEPTH, pack_columns, 0)
    pl.when(right)(y_up.start)
    pl.when(left)(y_dn.start)

    for has, copy, buf in ((up, x_up, row_halo.at[0]), (down, x_dn, row_halo.at[1]), (left, y_up, halo.at[0]), (right, y_dn, halo.at[1])):
        pl.when(has)(copy.wait_recv)

        @pl.when(jnp.logical_not(has))
        def _(buf=buf):
            buf[...] = jnp.zeros(buf.shape, BF16)

    pl.when(front)(z_up.wait_recv)
    pl.when(back)(z_dn.wait_recv)

    def unpack_rows(c, _):
        layers = pl.ds(2 + 8 * c, 8)
        at = pl.ds(pl.multiple_of(16 * c, 16), 16)
        for side, row in ((0, 0), (1, X + EDGE)):
            tiles = jnp.dot(unrow_mat[side], row_halo[side, at], preferred_element_type=F32)
            cells[layers, row : row + 16] = tiles.astype(BF16).reshape(8, 16, Y)
        return 0

    lax.fori_loop(0, Z // 8, unpack_rows, 0)

    slots = ((gy0, g0), (gy1, g1))

    def place(n):
        return lax.rem(me + 1 + (n >> 3), DEPTH), n & 7

    def slopes_y(n, slot):
        b, c = place(n)
        rows = pl.ds(pl.multiple_of(ROWS * b, ROWS), ROWS)
        inner = pl.ds(pl.multiple_of(EDGE + ROWS * b, EDGE), ROWS)
        sides = jnp.concatenate([halo[0, rows], halo[1, rows]], axis=1)
        layer_of = (lax.broadcasted_iota(jnp.int32, (ROWS, 256), 1) & 127) >> 1
        outer = jnp.stack([jnp.where(layer_of == 8 * c + i, sides, jnp.zeros_like(sides)) for i in range(8)])
        tiles = cells[pl.ds(2 + 8 * c, 8), inner].reshape(8 * ROWS, Y)
        gy = jnp.dot(tiles, y_mat[:Y], preferred_element_type=F32)
        gy += jnp.dot(outer.reshape(8 * ROWS, 256), y_mat[Y:], preferred_element_type=F32)
        slots[slot][0][...] = gy.reshape(8, ROWS, Y)

    def slopes_zx(n, slot, j):
        b, c = place(n)
        z = 8 * c + 2 * j
        wide = pl.ds(pl.multiple_of(ROWS * b, ROWS), ROWS + 2 * EDGE)
        inner = pl.ds(pl.multiple_of(EDGE + ROWS * b, EDGE), ROWS)
        tiles = [cells[z, inner], cells[z + 1, inner], cells[z + 2, wide], cells[z + 3, wide], cells[z + 4, inner], cells[z + 5, inner]]
        g = jnp.dot(zx_mat[...], jnp.concatenate(tiles, axis=0), preferred_element_type=F32)
        slots[slot][1][:, 2 * j : 2 * j + 2] = g.reshape(3, 2, ROWS, Y)

    def march(n, slot, s):
        b, c = place(n)
        gy_ref, g_ref = slots[slot]
        row, lane = (s // 2) * 16, (s % 2) * 128
        rs, ls = slice(row, row + 16), slice(lane, lane + 128)
        inner = pl.ds(pl.multiple_of(EDGE + ROWS * b + row, EDGE), 16)
        t, w_sum, r_sum, g_sum = (parts[b, k, rs, ls] for k in range(4))
        for i in range(8):
            d = cells[2 + 8 * c + i, inner, ls].astype(F32)
            gx, gz, gy = g_ref[0, i, rs, ls], g_ref[1, i, rs, ls], gy_ref[i, rs, ls]
            s25 = g_ref[2, i, rs, ls] + 16.0 * gy
            n2 = gx * gx + gz * gz + (gy * gy + 144.0)
            bright = jnp.abs(s25) * lax.rsqrt(n2) + BASE
            grow = jnp.exp2(d * EXP2_2D)
            k5 = grow + pltpu.reciprocal(grow, approx=True)
            t_next = t * jnp.exp2(k5 * EXP2_K)
            w = (t - t_next) * bright
            t = t_next
            w_sum = w_sum + w
            r_sum = r_sum + w * jnp.tanh(d)
            g_sum = g_sum + w * jnp.exp2(d * (d * EXP2_SQ))
        for k, v in enumerate((t, w_sum, r_sum, g_sum)):
            parts[b, k, rs, ls] = v

    def send(b):
        return pltpu.make_async_remote_copy(
            src_ref=parts.at[b], dst_ref=got.at[me], send_sem=send_sem.at[b], recv_sem=recv_sem.at[me],
            device_id={"depth": b}, device_id_type=MESH,
        )

    slopes_y(0, 0)
    for j in range(4):
        slopes_zx(0, 0, j)

    def pair(k, _):
        b = lax.rem(me + 1 + (k >> 2), DEPTH)

        @pl.when((k & 3) == 0)
        def _():
            parts[b, 0] = jnp.ones((ROWS, Y), F32)
            for i in (1, 2, 3):
                parts[b, i] = jnp.zeros((ROWS, Y), F32)

        for h in range(2):
            n = 2 * k + h
            slopes_y(n + 1, 1 - h)
            for s in range(4):
                slopes_zx(n + 1, 1 - h, s)
                march(n, h, s)

        @pl.when(jnp.logical_and((k & 3) == 3, k < 4 * DEPTH - 4))
        def _():
            send(b).start()

        return 0

    lax.fori_loop(0, 4 * DEPTH, pair, 0)

    got[me] = parts[me]
    for step in range(1, DEPTH):
        src = lax.rem(me + step, DEPTH)
        pltpu.make_async_remote_copy(
            src_ref=parts.at[src], dst_ref=got.at[src], send_sem=send_sem.at[src], recv_sem=recv_sem.at[src],
            device_id={"depth": src}, device_id_type=MESH,
        ).wait_recv()

    through = got[0, 0]
    w_sum, r_sum, g_sum = got[0, 1], got[0, 2], got[0, 3]
    for i in range(1, DEPTH):
        w_sum += through * got[i, 1]
        r_sum += through * got[i, 2]
        g_sum += through * got[i, 3]
        through = through * got[i, 0]
    out_ref[0] = (w_sum + r_sum) * (0.5 * 0.7 / 25.0)
    out_ref[1] = g_sum * (0.7 / 25.0)
    out_ref[2] = (w_sum - r_sum) * (0.5 * 0.7 / 25.0)
    out_ref[3] = 1.0 - through

    for step in range(1, DEPTH):
        send(lax.rem(me + step, DEPTH)).wait_send()
    for has, copy in ((back, z_up), (front, z_dn), (down, x_up), (up, x_dn), (right, y_up), (left, y_dn)):
        pl.when(has)(copy.wait_send)


def on_device(density):
    rows = pick_rows()
    mats = [jnp.asarray(m, BF16) for m in (along_y(), along_zx(), pick_columns(), rows, rows[::-1].transpose(0, 2, 1))]
    vmem, dma = pl.BlockSpec(memory_space=pltpu.VMEM), pltpu.SemaphoreType.DMA
    return pl.pallas_call(
        kernel,
        out_shape=jax.ShapeDtypeStruct((4, ROWS, Y), F32),
        in_specs=[pl.BlockSpec(memory_space=pl.ANY)] + [vmem] * 5,
        out_specs=vmem,
        scratch_shapes=[
            pltpu.VMEM((Z + 4, X + 2 * EDGE, Y), BF16),
            pltpu.VMEM((2, X, 128), BF16),
            pltpu.VMEM((2, X, 128), BF16),
            pltpu.VMEM((2, 2 * Z, Y), BF16),
            pltpu.VMEM((2, 2 * Z, Y), BF16),
            pltpu.VMEM((DEPTH, 4, ROWS, Y), F32),
            pltpu.VMEM((DEPTH, 4, ROWS, Y), F32),
        ]
        + [pltpu.VMEM((8, ROWS, Y), F32), pltpu.VMEM((3, 8, ROWS, Y), F32)] * 2
        + [dma((DEPTH,))]
        + [dma((2,))] * 6
        + [dma((DEPTH,))] * 2,
        compiler_params=pltpu.CompilerParams(collective_id=0, has_side_effects=True, vmem_limit_bytes=48 << 20),
        name="render",
    )(density, *mats)


def solution(mesh):
    return jax.shard_map(
        on_device,
        mesh=mesh,
        in_specs=(P("depth", "ix", "iy"),),
        out_specs=P(None, ("ix", "depth"), "iy"),
        check_vma=False,
    )
```

time: 417 us -> 57.8 us (0.14)
  other arithmetic: 281 us -> 0 us
  waiting for transfers between devices: 71.3 us -> 0 us
  Pallas kernels: 0 us -> 52.6 us
  local copies, waits for them, and re-layouts: 32.7 us -> 4.94 us
  starting transfers between devices: 16 us -> 0 us
  between operations: 13.5 us -> 0.01 us
    another operation x3 -> x0, other arithmetic: 251 us -> none  [the longest x1 250 us: shade_brick(): optical_before = jnp.cumsum(extinct, axis=0) - extinct]
    pallas_call x0 -> x1, Pallas kernels: none -> 52.6 us  [on_device(): pl.pallas_call(kernel, out_shape=jax.ShapeDtypeStruct((4, ROWS, Y), F32),...]
    reduce_scatter x1 -> x0, waiting for transfers between devices: 34.9 us -> none  [on_device(): image = lax.psum_scatter(layers, 'depth', scatter_dimension=1, tiled=True)]
    all_gather x1 -> x0, waiting for transfers between devices: 30.6 us -> none  [prefix(): gathered = lax.all_gather(part, axis)]
    convert_element_type x1 -> x0, other arithmetic: 21.8 us -> none  [on_device(): padded.astype(jnp.float32)]
    slice x5 -> x0, local copies, waits for them, and re-layouts: 16.5 us -> none  [the longest x3 11.1 us: extended(): lax.slice_in_dim(cells, cells.shape[dim] - width, cells.shape[dim], axis=...]
    ppermute x6 -> x0, starting transfers between devices: 15.9 us -> none  [the longest x3 11.3 us: extended(): lax.ppermute(tail, axis, [(i, (i + 1) % count) for i in range(ends)])]
    ppermute x2 -> x0, local copies, waits for them, and re-layouts: 7.11 us -> none  [the longest x1 3.57 us: extended(): lax.ppermute(head, axis, [((i + 1) % count, i) for i in range(ends)])]
  transfers between devices with their start and end apart: 8 -> 0, of which waited for: 5 -> 0; matrix products, arithmetic and copies ran while one was open for 4% -> 0% of each run, Pallas kernels for 0% -> 0%
where the time goes in v1:
time: 57.8 us; the launch traced here: 57.5 us
  Pallas kernels  52.6 us (91%)
  local copies, waits for them, and re-layouts  4.94 us (9%)
    pallas_call x1, Pallas kernels, on_device(): pl.pallas_call(kernel, out_shape=jax.ShapeDtypeStruct((4, ROWS, Y), F32),...  52.6 us
    unnamed x11, local copies, waits for them, and re-layouts  4.94 us

profile of v1, /device:TPU:1, one launch (start us, length us, event | category | flops | bytes accessed | tf_op | source)
XLA Modules:
  0.0 57.5 jit_solution(15087082909119180764)
XLA Ops:
  0.0 0.0 copy-start
  0.0 0.9 %copy-done = bf16[512,256]{1,0:T(8,128)(2,1)S(1)} copy-done((bf16[512,256]{1,0:T(8,128)(2,1)S(1)}, bf16[512,256]{1,0:T(8,128)(2,1)}, u32[]{:S(2)}) %copy-start) | copy-done | bytes 262168
  1.0 0.0 copy-start.1
  1.0 0.9 %copy-done.1 = bf16[256,256]{1,0:T(8,128)(2,1)S(1)} copy-done((bf16[256,256]{1,0:T(8,128)(2,1)S(1)}, bf16[256,256]{1,0:T(8,128)(2,1)}, u32[]{:S(2)}) %copy-start.1) | copy-done | bytes 131096
  1.9 0.0 copy-start.2
  1.9 0.9 %copy-done.2 = bf16[192,256]{1,0:T(8,128)(2,1)S(1)} copy-done((bf16[192,256]{1,0:T(8,128)(2,1)S(1)}, bf16[192,256]{1,0:T(8,128)(2,1)}, u32[]{:S(2)}) %copy-start.2) | copy-done | bytes 98328
  2.7 0.0 copy-start.3
  2.8 0.8 %copy-done.3 = bf16[2,128,16]{2,1,0:T(8,128)(2,1)S(1)} copy-done((bf16[2,128,16]{2,1,0:T(8,128)(2,1)S(1)}, bf16[2,128,16]{2,1,0:T(8,128)(2,1)}, u32[]{:S(2)}) %copy-start.3) | copy-done | bytes 8216
  3.6 0.0 copy-start.4
  3.6 0.7 %copy-done.4 = bf16[2,16,128]{2,1,0:T(8,128)(2,1)S(1)} copy-done((bf16[2,16,128]{2,1,0:T(8,128)(2,1)S(1)}, bf16[2,16,128]{2,1,0:T(8,128)(2,1)}, u32[]{:S(2)}) %copy-start.4) | copy-done | bytes 8216
  4.3 52.6 %render.1 = f32[4,32,256]{2,1,0:T(8,128)S(1)} custom-call(bf16[64,256,256]{2,1,0:T(8,128)(2,1)} %x_ref.1, bf16[512,256]{1,0:T(8,128)(2,1)S(1)} %copy-done, bf16[192,256]{1,0:T(8,128)(2,1)S(1)} %copy-done.2, bf16[256,256]{1,0:T(8,128)(2,1)S(1)} %copy-done.1, bf16[2,16,128]{2,1,0:T(8,128)(2,1)S(1)} %copy-done.4, bf16[2,128,16]{2,1,0:T(8,128)(2,1)S(1)} %copy-done.3), custom_call_target="tpu_custom_call" | custom-call | tf_op jit(solution)/shard_map/render/pallas_call | solution.py:292
  56.9 0.7 %copy.8 = f32[4,32,256]{2,1,0:T(8,128)} copy(f32[4,32,256]{2,1,0:T(8,128)S(1)} %render.1) | data formatting | bytes 262144
Async XLA Ops:
  0.0 0.9 %copy-start = (bf16[512,256]{1,0:T(8,128)(2,1)S(1)}, bf16[512,256]{1,0:T(8,128)(2,1)}, u32[]{:S(2)}) copy-start(bf16[512,256]{1,0:T(8,128)(2,1)} %constant.10.clone.y_mat) | copy-start | bytes 786436
  1.0 0.9 %copy-start.1 = (bf16[256,256]{1,0:T(8,128)(2,1)S(1)}, bf16[256,256]{1,0:T(8,128)(2,1)}, u32[]{:S(2)}) copy-start(bf16[256,256]{1,0:T(8,128)(2,1)} %constant.12.clone.col_mat) | copy-start | bytes 393220
  1.9 0.9 %copy-start.2 = (bf16[192,256]{1,0:T(8,128)(2,1)S(1)}, bf16[192,256]{1,0:T(8,128)(2,1)}, u32[]{:S(2)}) copy-start(bf16[192,256]{1,0:T(8,128)(2,1)} %constant.11.clone.zx_mat) | copy-start | bytes 294916
  2.7 0.8 %copy-start.3 = (bf16[2,128,16]{2,1,0:T(8,128)(2,1)S(1)}, bf16[2,128,16]{2,1,0:T(8,128)(2,1)}, u32[]{:S(2)}) copy-start(bf16[2,128,16]{2,1,0:T(8,128)(2,1)} %constant.14.clone.unrow_mat) | copy-start | bytes 24580
  3.6 0.7 %copy-start.4 = (bf16[2,16,128]{2,1,0:T(8,128)(2,1)S(1)}, bf16[2,16,128]{2,1,0:T(8,128)(2,1)}, u32[]{:S(2)}) copy-start(bf16[2,16,128]{2,1,0:T(8,128)(2,1)} %constant.13.clone.row_mat) | copy-start | bytes 24580

commit v2 on v1

--- a/solution.py
+++ b/solution.py
@@ -17,58 +17,35 @@
 EXP2_K = float(-0.1 * np.log2(np.e) / NZ)
 EXP2_SQ = float(-np.log2(np.e))
 BASE = 25.0 * 0.3 / 0.7
-TAPS = ((1, 8.0), (-1, -8.0), (2, -1.0), (-2, 1.0))
-
-
-def along_y():
-    inner = np.zeros((Y, Y), np.float32)
-    outer = np.zeros((256, Y), np.float32)
-    for y in range(Y):
-        for step, tap in TAPS:
-            at = y + step
-            if 0 <= at < Y:
-                inner[at, y] = tap
-            elif at < 0:
-                outer[[2 * z + at + 2 for z in range(Z)], y] = tap
-            else:
-                outer[[128 + 2 * z + at - Y for z in range(Z)], y] = tap
-    return np.concatenate([inner, outer])
-
-
-def along_zx():
-    start = (0, 32, 64 + 16, 128 + 16, 192, 224)
-    out = np.zeros((3, 2, ROWS, 256), np.float32)
-    for layer in range(2):
-        for row in range(ROWS):
-            for step, tap in TAPS:
-                across = start[layer + 2] + row + step
-                behind = start[layer + 2 + step] + row
-                out[0, layer, row, across] += tap
-                out[1, layer, row, behind] += tap
-                out[2, layer, row, across] += 15 * tap
-                out[2, layer, row, behind] += 12 * tap
-    return out.reshape(6 * ROWS, 256)
-
-
-def pick_columns():
-    out = np.zeros((Y, 256), np.float32)
-    for lane in range(256):
-        out[(0 if lane < 128 else Y - 2) + lane % 2, lane] = 1
-    return out
-
-
-def pick_rows():
-    out = np.zeros((2, 16, 128), np.float32)
-    for layer in range(8):
-        for row in range(2):
-            out[0, 2 * layer + row, 16 * layer + row] = 1
-            out[1, 2 * layer + row, 16 * layer + 14 + row] = 1
-    return out
+
+
+def tap(step):
+    near = jnp.where(step == 1, 8.0, jnp.where(step == -1, -8.0, 0.0))
+    return jnp.where(step == 2, -1.0, jnp.where(step == -2, 1.0, near))
+
+
+def fill_matrices(y_mat, zx_mat, pick, spread):
+    k, y = (lax.broadcasted_iota(jnp.int32, (256, Y), i) for i in (0, 1))
+    y_mat[:256] = tap(k - y).astype(BF16)
+    y_mat[256:] = tap(jnp.where(k < 128, (k & 1) - 2, Y + (k & 1)) - y).astype(BF16)
+    m, c = (lax.broadcasted_iota(jnp.int32, (2 * ROWS, 256), i) for i in (0, 1))
+    layer, row = m >> 5, m & 31
+    at = jnp.where(c < 64, c >> 5, jnp.where(c < 192, 1 + (c >> 6), (c >> 5) - 2))
+    across = jnp.where((c >= 64) & (c < 192), (c & 63) - EDGE, c & 31)
+    gx = jnp.where(at == layer + 2, tap(across - row), 0.0)
+    gz = jnp.where(across == row, tap(at - 2 - layer), 0.0)
+    for i, g in enumerate((gx, gz, 15.0 * gx + 12.0 * gz)):
+        zx_mat[2 * ROWS * i : 2 * ROWS * (i + 1)] = g.astype(BF16)
+    m, c = (lax.broadcasted_iota(jnp.int32, (16, 128), i) for i in (0, 1))
+    o, q = (lax.broadcasted_iota(jnp.int32, (128, 16), i) for i in (0, 1))
+    for side, start in ((0, 0), (1, 14)):
+        pick[side] = jnp.where(((c >> 4) == (m >> 1)) & ((c & 15) == start + (m & 1)), 1.0, 0.0).astype(BF16)
+        spread[1 - side] = jnp.where(((o >> 4) == (q >> 1)) & ((o & 15) == start + (q & 1)), 1.0, 0.0).astype(BF16)
 
 
 def kernel(
-    x_ref, y_mat, zx_mat, col_mat, row_mat, unrow_mat, out_ref,
-    cells, halo, pack, row_pack, row_halo, parts, got, gy0, g0, gy1, g1,
+    x_ref, out_ref,
+    y_mat, zx_mat, pick, spread, cells, halo, pack, row_pack, row_halo, parts, got, gy0, g0, gy1, g1,
     load_sem, z_send, z_recv, x_send, x_recv, y_send, y_recv, send_sem, recv_sem,
 ):
     me = lax.axis_index("depth")
@@ -83,8 +60,8 @@
         inner = pl.ds(pl.multiple_of(EDGE + ROWS * b, EDGE), ROWS)
         return pltpu.make_async_copy(x_ref.at[:, rows], cells.at[pl.ds(2, Z), inner], load_sem.at[b])
 
-    for b in range(DEPTH):
-        load(b).start()
+    for i in range(DEPTH):
+        load(lax.rem(me + 1 + i, DEPTH)).start()
 
     barrier = pltpu.get_barrier_semaphore()
     for step in range(1, DEPTH):
@@ -105,8 +82,17 @@
     z_dn = remote(x_ref.at[pl.ds(0, 2)], cells.at[pl.ds(Z + 2, 2), body], z_send, z_recv, 1, "depth", lax.rem(me + DEPTH - 1, DEPTH))
     x_up = remote(row_pack.at[1], row_halo.at[0], x_send, x_recv, 0, "ix", lax.rem(ix + 1, n_ix))
     x_dn = remote(row_pack.at[0], row_halo.at[1], x_send, x_recv, 1, "ix", lax.rem(ix + n_ix - 1, n_ix))
-    y_up = remote(pack.at[1], halo.at[0], y_send, y_recv, 0, "iy", lax.rem(iy + 1, n_iy))
-    y_dn = remote(pack.at[0], halo.at[1], y_send, y_recv, 1, "iy", lax.rem(iy + n_iy - 1, n_iy))
+
+    def y_copies(b):
+        low = pltpu.make_async_remote_copy(
+            src_ref=pack.at[1, b], dst_ref=halo.at[0, b], send_sem=y_send.at[0, b], recv_sem=y_recv.at[0, b],
+            device_id={"iy": lax.rem(iy + 1, n_iy)}, device_id_type=MESH,
+        )
+        high = pltpu.make_async_remote_copy(
+            src_ref=pack.at[0, b], dst_ref=halo.at[1, b], send_sem=y_send.at[1, b], recv_sem=y_recv.at[1, b],
+            device_id={"iy": lax.rem(iy + n_iy - 1, n_iy)}, device_id_type=MESH,
+        )
+        return low, high
 
     pl.when(back)(z_up.start)
     pl.when(front)(z_dn.start)
@@ -119,61 +105,74 @@
     def _():
         cells[Z + 2 : Z + 4] = jnp.zeros((2,) + cells.shape[1:], BF16)
 
-    for b in range(DEPTH):
+
+    fill_matrices(y_mat, zx_mat, pick, spread)
+    for side, has in ((0, left), (1, right)):
+
+        @pl.when(jnp.logical_not(has))
+        def _(side=side):
+            halo[side] = jnp.zeros(halo.shape[1:], BF16)
+
+    for side, has in ((0, up), (1, down)):
+
+        @pl.when(jnp.logical_not(has))
+        def _(side=side):
+            row_halo[side] = jnp.zeros(row_halo.shape[1:], BF16)
+
+    lane = lax.broadcasted_iota(jnp.int32, (16, 128), 1)
+
+    def pack_columns(b, half):
+        rows = pl.ds(pl.multiple_of(EDGE + ROWS * b + 16 * half, EDGE), 16)
+        first, last = jnp.zeros((16, 128), F32), jnp.zeros((16, 128), F32)
+        for z in range(Z):
+            ends = jnp.where(lane < 2, cells[2 + z, rows, :128].astype(F32), cells[2 + z, rows, Y - 128 :].astype(F32))
+            moved = pltpu.roll(ends, 2 * z, axis=1) if z else ends
+            first = jnp.where(lane >> 1 == z, moved, first)
+            last = jnp.where(lane >> 1 == (z + 63) & 63, moved, last)
+        last = pltpu.roll(last, 2, axis=1)
+        at = pl.ds(pl.multiple_of(16 * half, 16), 16)
+        pack[0, b, at] = first.astype(BF16)
+        pack[1, b, at] = last.astype(BF16)
+
+    def pack_block(i, _):
+        b = lax.rem(me + 1 + i, DEPTH)
         load(b).wait()
 
-    def pack_rows(c, _):
-        layers = pl.ds(2 + 8 * c, 8)
-        at = pl.ds(pl.multiple_of(16 * c, 16), 16)
-        for side, row in ((0, EDGE), (1, X)):
-            tiles = cells[layers, row : row + 16].reshape(128, Y)
-            row_pack[side, at] = jnp.dot(row_mat[side], tiles, preferred_element_type=F32).astype(BF16)
+        def one(half, _):
+            pack_columns(b, half)
+            return 0
+
+        lax.fori_loop(0, 2, one, 0)
+        low, high = y_copies(b)
+        pl.when(right)(low.start)
+        pl.when(left)(high.start)
         return 0
 
-    lax.fori_loop(0, Z // 8, pack_rows, 0)
+    pack_block(0, 0)
+    lax.fori_loop(1, DEPTH, pack_block, 0)
+    for side, row in ((0, EDGE), (1, X)):
+        for c in range(Z // 8):
+            tiles = cells[2 + 8 * c : 10 + 8 * c, row : row + 16].reshape(128, Y)
+            picked = jnp.dot(pick[side], tiles, preferred_element_type=F32)
+            row_pack[side, 16 * c : 16 * c + 16] = picked.astype(BF16)
     pl.when(down)(x_up.start)
     pl.when(up)(x_dn.start)
 
-    def pack_columns(b, _):
-        rows = pl.ds(pl.multiple_of(EDGE + ROWS * b, EDGE), ROWS)
-        layer_of = (lax.broadcasted_iota(jnp.int32, (ROWS, 256), 1) & 127) >> 1
-
-        def chunk(c, total):
-            tiles = cells[pl.ds(2 + 8 * c, 8), rows].reshape(8 * ROWS, Y)
-            picked = jnp.dot(tiles, col_mat[...], preferred_element_type=F32).reshape(8, ROWS, 256)
-            for i in range(8):
-                total = jnp.where(layer_of == 8 * c + i, picked[i], total)
-            return total
-
-        total = lax.fori_loop(0, Z // 8, chunk, jnp.zeros((ROWS, 256), F32)).astype(BF16)
-        at = pl.ds(pl.multiple_of(ROWS * b, ROWS), ROWS)
-        pack[0, at] = total[:, :128]
-        pack[1, at] = total[:, 128:]
-        return 0
-
-    lax.fori_loop(0, DEPTH, pack_columns, 0)
-    pl.when(right)(y_up.start)
-    pl.when(left)(y_dn.start)
-
-    for has, copy, buf in ((up, x_up, row_halo.at[0]), (down, x_dn, row_halo.at[1]), (left, y_up, halo.at[0]), (right, y_dn, halo.at[1])):
-        pl.when(has)(copy.wait_recv)
-
-        @pl.when(jnp.logical_not(has))
-        def _(buf=buf):
-            buf[...] = jnp.zeros(buf.shape, BF16)
-
     pl.when(front)(z_up.wait_recv)
     pl.when(back)(z_dn.wait_recv)
-
-    def unpack_rows(c, _):
-        layers = pl.ds(2 + 8 * c, 8)
-        at = pl.ds(pl.multiple_of(16 * c, 16), 16)
-        for side, row in ((0, 0), (1, X + EDGE)):
-            tiles = jnp.dot(unrow_mat[side], row_halo[side, at], preferred_element_type=F32)
-            cells[layers, row : row + 16] = tiles.astype(BF16).reshape(8, 16, Y)
-        return 0
-
-    lax.fori_loop(0, Z // 8, unpack_rows, 0)
+    pl.when(up)(x_up.wait_recv)
+    pl.when(down)(x_dn.wait_recv)
+    for side, row in ((0, 0), (1, X + EDGE)):
+        for c in range(Z // 8):
+            tiles = jnp.dot(spread[side], row_halo[side, 16 * c : 16 * c + 16], preferred_element_type=F32)
+            cells[2 + 8 * c : 10 + 8 * c, row : row + 16] = tiles.astype(BF16).reshape(8, 16, Y)
+
+    def wait_sides(b):
+        low, high = y_copies(b)
+        pl.when(left)(low.wait_recv)
+        pl.when(right)(high.wait_recv)
+
+    wait_sides(lax.rem(me + 1, DEPTH))
 
     slots = ((gy0, g0), (gy1, g1))
 
@@ -182,9 +181,8 @@
 
     def slopes_y(n, slot):
         b, c = place(n)
-        rows = pl.ds(pl.multiple_of(ROWS * b, ROWS), ROWS)
         inner = pl.ds(pl.multiple_of(EDGE + ROWS * b, EDGE), ROWS)
-        sides = jnp.concatenate([halo[0, rows], halo[1, rows]], axis=1)
+        sides = jnp.concatenate([halo[0, b], halo[1, b]], axis=1)
         layer_of = (lax.broadcasted_iota(jnp.int32, (ROWS, 256), 1) & 127) >> 1
         outer = jnp.stack([jnp.where(layer_of == 8 * c + i, sides, jnp.zeros_like(sides)) for i in range(8)])
         tiles = cells[pl.ds(2 + 8 * c, 8), inner].reshape(8 * ROWS, Y)
@@ -244,6 +242,10 @@
             for i in (1, 2, 3):
                 parts[b, i] = jnp.zeros((ROWS, Y), F32)
 
+        @pl.when(jnp.logical_and((k & 3) == 3, k < 4 * DEPTH - 1))
+        def _():
+            wait_sides(lax.rem(b + 1, DEPTH))
+
         for h in range(2):
             n = 2 * k + h
             slopes_y(n + 1, 1 - h)
@@ -281,23 +283,29 @@
 
     for step in range(1, DEPTH):
         send(lax.rem(me + step, DEPTH)).wait_send()
-    for has, copy in ((back, z_up), (front, z_dn), (down, x_up), (up, x_dn), (right, y_up), (left, y_dn)):
+    for has, copy in ((back, z_up), (front, z_dn), (down, x_up), (up, x_dn)):
         pl.when(has)(copy.wait_send)
+    for b in range(DEPTH):
+        low, high = y_copies(b)
+        pl.when(right)(low.wait_send)
+        pl.when(left)(high.wait_send)
 
 
 def on_device(density):
-    rows = pick_rows()
-    mats = [jnp.asarray(m, BF16) for m in (along_y(), along_zx(), pick_columns(), rows, rows[::-1].transpose(0, 2, 1))]
     vmem, dma = pl.BlockSpec(memory_space=pltpu.VMEM), pltpu.SemaphoreType.DMA
     return pl.pallas_call(
         kernel,
         out_shape=jax.ShapeDtypeStruct((4, ROWS, Y), F32),
-        in_specs=[pl.BlockSpec(memory_space=pl.ANY)] + [vmem] * 5,
+        in_specs=[pl.BlockSpec(memory_space=pl.ANY)],
         out_specs=vmem,
         scratch_shapes=[
+            pltpu.VMEM((Y + 256, Y), BF16),
+            pltpu.VMEM((6 * ROWS, 256), BF16),
+            pltpu.VMEM((2, 16, 128), BF16),
+            pltpu.VMEM((2, 128, 16), BF16),
             pltpu.VMEM((Z + 4, X + 2 * EDGE, Y), BF16),
-            pltpu.VMEM((2, X, 128), BF16),
-            pltpu.VMEM((2, X, 128), BF16),
+            pltpu.VMEM((2, DEPTH, ROWS, 128), BF16),
+            pltpu.VMEM((2, DEPTH, ROWS, 128), BF16),
             pltpu.VMEM((2, 2 * Z, Y), BF16),
             pltpu.VMEM((2, 2 * Z, Y), BF16),
             pltpu.VMEM((DEPTH, 4, ROWS, Y), F32),
@@ -305,11 +313,12 @@
         ]
         + [pltpu.VMEM((8, ROWS, Y), F32), pltpu.VMEM((3, 8, ROWS, Y), F32)] * 2
         + [dma((DEPTH,))]
-        + [dma((2,))] * 6
+        + [dma((2,))] * 4
+        + [dma((2, DEPTH))] * 2
         + [dma((DEPTH,))] * 2,
-        compiler_params=pltpu.CompilerParams(collective_id=0, has_side_effects=True, vmem_limit_bytes=48 << 20),
+        compiler_params=pltpu.CompilerParams(collective_id=0, has_side_effects=True, vmem_limit_bytes=58 << 20),
         name="render",
-    )(density, *mats)
+    )(density)
 
 
 def solution(mesh):

time: 57.8 us -> 44.1 us (0.76)
  Pallas kernels: 52.6 us -> 42.4 us
  local copies, waits for them, and re-layouts: 4.94 us -> 1.57 us
    pallas_call x1, Pallas kernels: 52.6 us -> 42.4 us  [on_device(): pl.pallas_call(kernel, out_shape=jax.ShapeDtypeStruct((4, ROWS, Y), F32),...]
    unnamed x11 -> x1, local copies, waits for them, and re-layouts: 4.94 us -> 1.57 us
where the time goes in v2:
time: 44.1 us; the launch traced here: 44 us
  Pallas kernels  42.4 us (96%)
  local copies, waits for them, and re-layouts  1.57 us (4%)
    pallas_call x1, Pallas kernels, on_device(): pl.pallas_call(kernel, out_shape=jax.ShapeDtypeStruct((4, ROWS, Y), F32),...  42.4 us
    unnamed x1, local copies, waits for them, and re-layouts  1.57 us

profile of v2, /device:TPU:1, one launch (start us, length us, event | category | flops | bytes accessed | tf_op | source)
XLA Modules:
  0.0 44.0 jit_solution(6571460215642069815)
XLA Ops:
  0.0 42.4 %render.1 = f32[4,32,256]{2,1,0:T(8,128)} custom-call(bf16[64,256,256]{2,1,0:T(8,128)(2,1)} %x_ref.1), custom_call_target="tpu_custom_call" | custom-call | tf_op jit(solution)/shard_map/render/pallas_call | solution.py:296
  42.4 1.6 %copy.3 = f32[4,32,256]{2,1,0:T(8,128)} copy(f32[4,32,256]{2,1,0:T(8,128)} %render.1) | data formatting | bytes 262144

commit v3 on v2

--- a/solution.py
+++ b/solution.py
@@ -45,8 +45,8 @@
 
 def kernel(
     x_ref, out_ref,
-    y_mat, zx_mat, pick, spread, cells, halo, pack, row_pack, row_halo, parts, got, gy0, g0, gy1, g1,
-    load_sem, z_send, z_recv, x_send, x_recv, y_send, y_recv, send_sem, recv_sem,
+    y_mat, zx_mat, pick, spread, cells, halo, pack, row_pack, row_halo, parts, got,
+    load_sem, z_send, z_recv, x_send, x_recv, y_send, y_recv, send_sem, recv_sem, *slopes,
 ):
     me = lax.axis_index("depth")
     ix, iy = lax.axis_index("ix"), lax.axis_index("iy")
@@ -174,21 +174,23 @@
 
     wait_sides(lax.rem(me + 1, DEPTH))
 
-    slots = ((gy0, g0), (gy1, g1))
+    slots = tuple(zip(slopes[:4], slopes[4:]))
 
     def place(n):
         return lax.rem(me + 1 + (n >> 3), DEPTH), n & 7
 
-    def slopes_y(n, slot):
+    def slopes_y(n, first):
         b, c = place(n)
         inner = pl.ds(pl.multiple_of(EDGE + ROWS * b, EDGE), ROWS)
         sides = jnp.concatenate([halo[0, b], halo[1, b]], axis=1)
         layer_of = (lax.broadcasted_iota(jnp.int32, (ROWS, 256), 1) & 127) >> 1
-        outer = jnp.stack([jnp.where(layer_of == 8 * c + i, sides, jnp.zeros_like(sides)) for i in range(8)])
-        tiles = cells[pl.ds(2 + 8 * c, 8), inner].reshape(8 * ROWS, Y)
+        outer = jnp.stack([jnp.where(layer_of == 8 * c + i, sides, jnp.zeros_like(sides)) for i in range(16)])
+        tiles = cells[pl.ds(2 + 8 * c, 16), inner].reshape(16 * ROWS, Y)
         gy = jnp.dot(tiles, y_mat[:Y], preferred_element_type=F32)
-        gy += jnp.dot(outer.reshape(8 * ROWS, 256), y_mat[Y:], preferred_element_type=F32)
-        slots[slot][0][...] = gy.reshape(8, ROWS, Y)
+        gy += jnp.dot(outer.reshape(16 * ROWS, 256), y_mat[Y:], preferred_element_type=F32)
+        gy = gy.reshape(2, 8, ROWS, Y)
+        slots[first][0][...] = gy[0]
+        slots[first + 1][0][...] = gy[1]
 
     def slopes_zx(n, slot, j):
         b, c = place(n)
@@ -230,36 +232,40 @@
         )
 
     slopes_y(0, 0)
-    for j in range(4):
-        slopes_zx(0, 0, j)
-
-    def pair(k, _):
-        b = lax.rem(me + 1 + (k >> 2), DEPTH)
-
-        @pl.when((k & 3) == 0)
+    for q in range(2):
+        for j in range(4):
+            slopes_zx(q, q, j)
+
+    def half_block(k, _):
+        b = lax.rem(me + 1 + (k >> 1), DEPTH)
+
+        @pl.when((k & 1) == 0)
         def _():
             parts[b, 0] = jnp.ones((ROWS, Y), F32)
             for i in (1, 2, 3):
                 parts[b, i] = jnp.zeros((ROWS, Y), F32)
 
-        @pl.when(jnp.logical_and((k & 3) == 3, k < 4 * DEPTH - 1))
+        @pl.when(jnp.logical_and((k & 1) == 1, k < 2 * DEPTH - 1))
         def _():
             wait_sides(lax.rem(b + 1, DEPTH))
 
         for h in range(2):
-            n = 2 * k + h
-            slopes_y(n + 1, 1 - h)
-            for s in range(4):
-                slopes_zx(n + 1, 1 - h, s)
-                march(n, h, s)
-
-        @pl.when(jnp.logical_and((k & 3) == 3, k < 4 * DEPTH - 4))
+            @pl.when(k + me >= 0)
+            def _(h=h):
+                n = 4 * k + 2 * h
+                use, fill = 2 * h, 2 - 2 * h
+                slopes_y(n + 2, fill)
+                for i in range(8):
+                    slopes_zx(n + 2 + i // 4, fill + i // 4, i % 4)
+                    march(n + i % 2, use + i % 2, i // 2)
+
+        @pl.when(jnp.logical_and((k & 1) == 1, k < 2 * DEPTH - 2))
         def _():
             send(b).start()
 
         return 0
 
-    lax.fori_loop(0, 4 * DEPTH, pair, 0)
+    lax.fori_loop(0, 2 * DEPTH, half_block, 0)
 
     got[me] = parts[me]
     for step in range(1, DEPTH):
@@ -311,12 +317,13 @@
             pltpu.VMEM((DEPTH, 4, ROWS, Y), F32),
             pltpu.VMEM((DEPTH, 4, ROWS, Y), F32),
         ]
-        + [pltpu.VMEM((8, ROWS, Y), F32), pltpu.VMEM((3, 8, ROWS, Y), F32)] * 2
         + [dma((DEPTH,))]
         + [dma((2,))] * 4
         + [dma((2, DEPTH))] * 2
-        + [dma((DEPTH,))] * 2,
-        compiler_params=pltpu.CompilerParams(collective_id=0, has_side_effects=True, vmem_limit_bytes=58 << 20),
+        + [dma((DEPTH,))] * 2
+        + [pltpu.VMEM((8, ROWS, Y), F32)] * 4
+        + [pltpu.VMEM((3, 8, ROWS, Y), F32)] * 4,
+        compiler_params=pltpu.CompilerParams(collective_id=0, has_side_effects=True, vmem_limit_bytes=48 << 20),
         name="render",
     )(density)
 

time: 44.1 us -> 41.1 us (0.932)
  Pallas kernels: 42.4 us -> 40.4 us
  local copies, waits for them, and re-layouts: 1.57 us -> 0.66 us
    pallas_call x1, Pallas kernels: 42.4 us -> 40.4 us  [on_device(): pl.pallas_call(kernel, out_shape=jax.ShapeDtypeStruct((4, ROWS, Y), F32),...]
    unnamed x1, local copies, waits for them, and re-layouts: 1.57 us -> 0.66 us
where the time goes in v3:
time: 41.1 us; the launch traced here: 41 us
  Pallas kernels  40.4 us (98%)
  local copies, waits for them, and re-layouts  0.66 us (2%)
    pallas_call x1, Pallas kernels, on_device(): pl.pallas_call(kernel, out_shape=jax.ShapeDtypeStruct((4, ROWS, Y), F32),...  40.4 us

profile of v3, /device:TPU:1, one launch (start us, length us, event | category | flops | bytes accessed | tf_op | source)
XLA Modules:
  0.0 41.0 jit_solution(16697656674259544012)
XLA Ops:
  0.0 40.4 %render.1 = f32[4,32,256]{2,1,0:T(8,128)S(1)} custom-call(bf16[64,256,256]{2,1,0:T(8,128)(2,1)} %x_ref.1), custom_call_target="tpu_custom_call" | custom-call | tf_op jit(solution)/shard_map/render/pallas_call | solution.py:302
  40.4 0.7 %copy.3 = f32[4,32,256]{2,1,0:T(8,128)} copy(f32[4,32,256]{2,1,0:T(8,128)S(1)} %render.1) | data formatting | bytes 262144

commit v4 on v3

--- a/solution.py
+++ b/solution.py
@@ -60,16 +60,14 @@
         inner = pl.ds(pl.multiple_of(EDGE + ROWS * b, EDGE), ROWS)
         return pltpu.make_async_copy(x_ref.at[:, rows], cells.at[pl.ds(2, Z), inner], load_sem.at[b])
 
-    for i in range(DEPTH):
-        load(lax.rem(me + 1 + i, DEPTH)).start()
-
     barrier = pltpu.get_barrier_semaphore()
     for step in range(1, DEPTH):
         pl.semaphore_signal(barrier, inc=1, device_id={"depth": lax.rem(me + step, DEPTH)}, device_id_type=MESH)
     for axis, at, count in (("ix", ix, n_ix), ("iy", iy, n_iy)):
         for step in (1, count - 1):
             pl.semaphore_signal(barrier, inc=1, device_id={axis: lax.rem(at + step, count)}, device_id_type=MESH)
-    pl.semaphore_wait(barrier, DEPTH - 1 + 4)
+    for i in range(DEPTH):
+        load(lax.rem(me + 1 + i, DEPTH)).start()
 
     def remote(src, dst, sems, recvs, k, axis, to):
         return pltpu.make_async_remote_copy(
@@ -77,9 +75,19 @@
             device_id={axis: to}, device_id_type=MESH,
         )
 
-    body = pl.ds(EDGE, X)
-    z_up = remote(x_ref.at[pl.ds(Z - 2, 2)], cells.at[pl.ds(0, 2), body], z_send, z_recv, 0, "depth", lax.rem(me + 1, DEPTH))
-    z_dn = remote(x_ref.at[pl.ds(0, 2)], cells.at[pl.ds(Z + 2, 2), body], z_send, z_recv, 1, "depth", lax.rem(me + DEPTH - 1, DEPTH))
+    def z_copies(b):
+        rows = pl.ds(pl.multiple_of(ROWS * b, ROWS), ROWS)
+        inner = pl.ds(pl.multiple_of(EDGE + ROWS * b, EDGE), ROWS)
+        low = pltpu.make_async_remote_copy(
+            src_ref=x_ref.at[pl.ds(Z - 2, 2), rows], dst_ref=cells.at[pl.ds(0, 2), inner], send_sem=z_send.at[0, b], recv_sem=z_recv.at[0, b],
+            device_id={"depth": lax.rem(me + 1, DEPTH)}, device_id_type=MESH,
+        )
+        high = pltpu.make_async_remote_copy(
+            src_ref=x_ref.at[pl.ds(0, 2), rows], dst_ref=cells.at[pl.ds(Z + 2, 2), inner], send_sem=z_send.at[1, b], recv_sem=z_recv.at[1, b],
+            device_id={"depth": lax.rem(me + DEPTH - 1, DEPTH)}, device_id_type=MESH,
+        )
+        return low, high
+
     x_up = remote(row_pack.at[1], row_halo.at[0], x_send, x_recv, 0, "ix", lax.rem(ix + 1, n_ix))
     x_dn = remote(row_pack.at[0], row_halo.at[1], x_send, x_recv, 1, "ix", lax.rem(ix + n_ix - 1, n_ix))
 
@@ -94,8 +102,6 @@
         )
         return low, high
 
-    pl.when(back)(z_up.start)
-    pl.when(front)(z_dn.start)
 
     @pl.when(jnp.logical_not(front))
     def _():
@@ -143,36 +149,47 @@
             return 0
 
         lax.fori_loop(0, 2, one, 0)
-        low, high = y_copies(b)
-        pl.when(right)(low.start)
-        pl.when(left)(high.start)
         return 0
 
-    pack_block(0, 0)
-    lax.fori_loop(1, DEPTH, pack_block, 0)
+    lax.fori_loop(0, DEPTH, pack_block, 0)
     for side, row in ((0, EDGE), (1, X)):
         for c in range(Z // 8):
             tiles = cells[2 + 8 * c : 10 + 8 * c, row : row + 16].reshape(128, Y)
             picked = jnp.dot(pick[side], tiles, preferred_element_type=F32)
             row_pack[side, 16 * c : 16 * c + 16] = picked.astype(BF16)
+
+    pl.semaphore_wait(barrier, DEPTH - 1 + 4)
+
+    def send_edges(i, _):
+        b = lax.rem(me + 1 + i, DEPTH)
+        for copies, to_high, to_low in ((z_copies(b), back, front), (y_copies(b), right, left)):
+            pl.when(to_high)(copies[0].start)
+            pl.when(to_low)(copies[1].start)
+        return 0
+
+    send_edges(0, 0)
     pl.when(down)(x_up.start)
     pl.when(up)(x_dn.start)
-
-    pl.when(front)(z_up.wait_recv)
-    pl.when(back)(z_dn.wait_recv)
-    pl.when(up)(x_up.wait_recv)
-    pl.when(down)(x_dn.wait_recv)
-    for side, row in ((0, 0), (1, X + EDGE)):
-        for c in range(Z // 8):
-            tiles = jnp.dot(spread[side], row_halo[side, 16 * c : 16 * c + 16], preferred_element_type=F32)
-            cells[2 + 8 * c : 10 + 8 * c, row : row + 16] = tiles.astype(BF16).reshape(8, 16, Y)
-
-    def wait_sides(b):
+    lax.fori_loop(1, DEPTH, send_edges, 0)
+
+    def wait_front(b):
         low, high = y_copies(b)
         pl.when(left)(low.wait_recv)
         pl.when(right)(high.wait_recv)
-
-    wait_sides(lax.rem(me + 1, DEPTH))
+        pl.when(front)(z_copies(b)[0].wait_recv)
+        for side, has, copy, at, row in ((0, up, x_up, 0, 0), (1, down, x_dn, DEPTH - 1, X + EDGE)):
+
+            @pl.when(b == at)
+            def _(side=side, has=has, copy=copy, row=row):
+                pl.when(has)(copy.wait_recv)
+                for c in range(Z // 8):
+                    tiles = jnp.dot(spread[side], row_halo[side, 16 * c : 16 * c + 16], preferred_element_type=F32)
+                    cells[2 + 8 * c : 10 + 8 * c, row : row + 16] = tiles.astype(BF16).reshape(8, 16, Y)
+
+    def wait_back(b):
+        pl.when(back)(z_copies(b)[1].wait_recv)
+
+    wait_front(lax.rem(me + 1, DEPTH))
 
     slots = tuple(zip(slopes[:4], slopes[4:]))
 
@@ -245,9 +262,13 @@
             for i in (1, 2, 3):
                 parts[b, i] = jnp.zeros((ROWS, Y), F32)
 
+        @pl.when((k & 1) == 1)
+        def _():
+            wait_back(b)
+
         @pl.when(jnp.logical_and((k & 1) == 1, k < 2 * DEPTH - 1))
         def _():
-            wait_sides(lax.rem(b + 1, DEPTH))
+            wait_front(lax.rem(b + 1, DEPTH))
 
         for h in range(2):
             @pl.when(k + me >= 0)
@@ -289,12 +310,16 @@
 
     for step in range(1, DEPTH):
         send(lax.rem(me + step, DEPTH)).wait_send()
-    for has, copy in ((back, z_up), (front, z_dn), (down, x_up), (up, x_dn)):
+    for has, copy in ((down, x_up), (up, x_dn)):
         pl.when(has)(copy.wait_send)
-    for b in range(DEPTH):
-        low, high = y_copies(b)
-        pl.when(right)(low.wait_send)
-        pl.when(left)(high.wait_send)
+
+    def sent_edges(b, _):
+        for copies, to_high, to_low in ((z_copies(b), back, front), (y_copies(b), right, left)):
+            pl.when(to_high)(copies[0].wait_send)
+            pl.when(to_low)(copies[1].wait_send)
+        return 0
+
+    lax.fori_loop(0, DEPTH, sent_edges, 0)
 
 
 def on_device(density):
@@ -318,7 +343,8 @@
             pltpu.VMEM((DEPTH, 4, ROWS, Y), F32),
         ]
         + [dma((DEPTH,))]
-        + [dma((2,))] * 4
+        + [dma((2, DEPTH))] * 2
+        + [dma((2,))] * 2
         + [dma((2, DEPTH))] * 2
         + [dma((DEPTH,))] * 2
         + [pltpu.VMEM((8, ROWS, Y), F32)] * 4

time: 41.1 us -> 38.5 us (0.937)
  Pallas kernels: 40.4 us -> 37.7 us
    pallas_call x1, Pallas kernels: 40.4 us -> 37.7 us  [on_device(): pl.pallas_call(kernel, out_shape=jax.ShapeDtypeStruct((4, ROWS, Y), F32),...]
where the time goes in v4:
time: 38.5 us; the launch traced here: 38.4 us
  Pallas kernels  37.7 us (98%)
  local copies, waits for them, and re-layouts  0.66 us (2%)
    pallas_call x1, Pallas kernels, on_device(): pl.pallas_call(kernel, out_shape=jax.ShapeDtypeStruct((4, ROWS, Y), F32),...  37.7 us

profile of v4, /device:TPU:1, one launch (start us, length us, event | category | flops | bytes accessed | tf_op | source)
XLA Modules:
  0.0 38.4 jit_solution(14863549721143058982)
XLA Ops:
  0.0 37.7 %render.1 = f32[4,32,256]{2,1,0:T(8,128)S(1)} custom-call(bf16[64,256,256]{2,1,0:T(8,128)(2,1)} %x_ref.1), custom_call_target="tpu_custom_call" | custom-call | tf_op jit(solution)/shard_map/render/pallas_call | solution.py:327
  37.7 0.7 %copy.3 = f32[4,32,256]{2,1,0:T(8,128)} copy(f32[4,32,256]{2,1,0:T(8,128)S(1)} %render.1) | data formatting | bytes 262144

commit v5 on v4

--- a/solution.py
+++ b/solution.py
@@ -13,10 +13,12 @@
 ROWS = X // DEPTH
 EDGE = 16
 NZ = 512
+LAG = 3
 EXP2_2D = float(2.0 * np.log2(np.e))
 EXP2_K = float(-0.1 * np.log2(np.e) / NZ)
 EXP2_SQ = float(-np.log2(np.e))
-BASE = 25.0 * 0.3 / 0.7
+SCALE = 0.7 * 16.0 / 25.0
+BASE = 0.3 / SCALE
 
 
 def tap(step):
@@ -34,7 +36,7 @@
     across = jnp.where((c >= 64) & (c < 192), (c & 63) - EDGE, c & 31)
     gx = jnp.where(at == layer + 2, tap(across - row), 0.0)
     gz = jnp.where(across == row, tap(at - 2 - layer), 0.0)
-    for i, g in enumerate((gx, gz, 15.0 * gx + 12.0 * gz)):
+    for i, g in enumerate((gx, gz, (15.0 / 16.0) * gx + (12.0 / 16.0) * gz)):
         zx_mat[2 * ROWS * i : 2 * ROWS * (i + 1)] = g.astype(BF16)
     m, c = (lax.broadcasted_iota(jnp.int32, (16, 128), i) for i in (0, 1))
     o, q = (lax.broadcasted_iota(jnp.int32, (128, 16), i) for i in (0, 1))
@@ -55,6 +57,10 @@
     up, down = ix > 0, ix < n_ix - 1
     left, right = iy > 0, iy < n_iy - 1
 
+    def block(i, at=me):
+        swap = jnp.where(at == 7, 1, jnp.where(at == 6, 2, 0))
+        return lax.rem(at + 1 + jnp.where(i <= swap, swap - i, i), DEPTH)
+
     def load(b):
         rows = pl.ds(pl.multiple_of(ROWS * b, ROWS), ROWS)
         inner = pl.ds(pl.multiple_of(EDGE + ROWS * b, EDGE), ROWS)
@@ -67,7 +73,7 @@
         for step in (1, count - 1):
             pl.semaphore_signal(barrier, inc=1, device_id={axis: lax.rem(at + step, count)}, device_id_type=MESH)
     for i in range(DEPTH):
-        load(lax.rem(me + 1 + i, DEPTH)).start()
+        load(block(i)).start()
 
     def remote(src, dst, sems, recvs, k, axis, to):
         return pltpu.make_async_remote_copy(
@@ -141,7 +147,7 @@
         pack[1, b, at] = last.astype(BF16)
 
     def pack_block(i, _):
-        b = lax.rem(me + 1 + i, DEPTH)
+        b = block(i)
         load(b).wait()
 
         def one(half, _):
@@ -158,43 +164,10 @@
             picked = jnp.dot(pick[side], tiles, preferred_element_type=F32)
             row_pack[side, 16 * c : 16 * c + 16] = picked.astype(BF16)
 
-    pl.semaphore_wait(barrier, DEPTH - 1 + 4)
-
-    def send_edges(i, _):
-        b = lax.rem(me + 1 + i, DEPTH)
-        for copies, to_high, to_low in ((z_copies(b), back, front), (y_copies(b), right, left)):
-            pl.when(to_high)(copies[0].start)
-            pl.when(to_low)(copies[1].start)
-        return 0
-
-    send_edges(0, 0)
-    pl.when(down)(x_up.start)
-    pl.when(up)(x_dn.start)
-    lax.fori_loop(1, DEPTH, send_edges, 0)
-
-    def wait_front(b):
-        low, high = y_copies(b)
-        pl.when(left)(low.wait_recv)
-        pl.when(right)(high.wait_recv)
-        pl.when(front)(z_copies(b)[0].wait_recv)
-        for side, has, copy, at, row in ((0, up, x_up, 0, 0), (1, down, x_dn, DEPTH - 1, X + EDGE)):
-
-            @pl.when(b == at)
-            def _(side=side, has=has, copy=copy, row=row):
-                pl.when(has)(copy.wait_recv)
-                for c in range(Z // 8):
-                    tiles = jnp.dot(spread[side], row_halo[side, 16 * c : 16 * c + 16], preferred_element_type=F32)
-                    cells[2 + 8 * c : 10 + 8 * c, row : row + 16] = tiles.astype(BF16).reshape(8, 16, Y)
-
-    def wait_back(b):
-        pl.when(back)(z_copies(b)[1].wait_recv)
-
-    wait_front(lax.rem(me + 1, DEPTH))
-
     slots = tuple(zip(slopes[:4], slopes[4:]))
 
     def place(n):
-        return lax.rem(me + 1 + (n >> 3), DEPTH), n & 7
+        return block(n >> 3), n & 7
 
     def slopes_y(n, first):
         b, c = place(n)
@@ -218,19 +191,67 @@
         g = jnp.dot(zx_mat[...], jnp.concatenate(tiles, axis=0), preferred_element_type=F32)
         slots[slot][1][:, 2 * j : 2 * j + 2] = g.reshape(3, 2, ROWS, Y)
 
-    def march(n, slot, s):
+    for j in range(1, 8):
+        slopes_zx(j // 4, j // 4, j % 4)
+
+    pl.semaphore_wait(barrier, DEPTH - 1 + 4)
+
+    def send_layers(i, _):
+        pl.when(back)(z_copies(block(i, me + 1))[0].start)
+        pl.when(front)(z_copies(block(i, me - 1))[1].start)
+        return 0
+
+    def send_columns(i, _):
+        low, high = y_copies(block(i))
+        pl.when(right)(low.start)
+        pl.when(left)(high.start)
+        return 0
+
+    send_columns(0, 0)
+    send_layers(0, 0)
+    pl.when(down)(x_up.start)
+    pl.when(up)(x_dn.start)
+
+    def send_rest(i, _):
+        send_columns(i, 0)
+        return send_layers(i, 0)
+
+    lax.fori_loop(1, DEPTH, send_rest, 0)
+
+    def wait_front(b):
+        low, high = y_copies(b)
+        pl.when(left)(low.wait_recv)
+        pl.when(right)(high.wait_recv)
+        pl.when(front)(z_copies(b)[0].wait_recv)
+        for side, has, copy, at, row in ((0, up, x_up, 0, 0), (1, down, x_dn, DEPTH - 1, X + EDGE)):
+
+            @pl.when(b == at)
+            def _(side=side, has=has, copy=copy, row=row):
+                pl.when(has)(copy.wait_recv)
+                for c in range(Z // 8):
+                    tiles = jnp.dot(spread[side], row_halo[side, 16 * c : 16 * c + 16], preferred_element_type=F32)
+                    cells[2 + 8 * c : 10 + 8 * c, row : row + 16] = tiles.astype(BF16).reshape(8, 16, Y)
+
+    def wait_back(b):
+        pl.when(back)(z_copies(b)[1].wait_recv)
+
+    wait_front(block(0))
+
+    def march(n, slot, s, after):
         b, c = place(n)
         gy_ref, g_ref = slots[slot]
         row, lane = (s // 2) * 16, (s % 2) * 128
         rs, ls = slice(row, row + 16), slice(lane, lane + 128)
         inner = pl.ds(pl.multiple_of(EDGE + ROWS * b + row, EDGE), 16)
         t, w_sum, r_sum, g_sum = (parts[b, k, rs, ls] for k in range(4))
+        for ref in after:
+            t = t + 0.0 * ref[rs, ls]
         for i in range(8):
             d = cells[2 + 8 * c + i, inner, ls].astype(F32)
             gx, gz, gy = g_ref[0, i, rs, ls], g_ref[1, i, rs, ls], gy_ref[i, rs, ls]
-            s25 = g_ref[2, i, rs, ls] + 16.0 * gy
+            along = g_ref[2, i, rs, ls] + gy
             n2 = gx * gx + gz * gz + (gy * gy + 144.0)
-            bright = jnp.abs(s25) * lax.rsqrt(n2) + BASE
+            bright = jnp.abs(along) * lax.rsqrt(n2) + BASE
             grow = jnp.exp2(d * EXP2_2D)
             k5 = grow + pltpu.reciprocal(grow, approx=True)
             t_next = t * jnp.exp2(k5 * EXP2_K)
@@ -248,45 +269,42 @@
             device_id={"depth": b}, device_id_type=MESH,
         )
 
+    slopes_zx(0, 0, 0)
     slopes_y(0, 0)
-    for q in range(2):
-        for j in range(4):
-            slopes_zx(q, q, j)
-
-    def half_block(k, _):
-        b = lax.rem(me + 1 + (k >> 1), DEPTH)
-
-        @pl.when((k & 1) == 0)
+
+    def turn(m, _):
+        i, quarter = m >> 2, m & 3
+        b = block(i)
+
+        @pl.when(quarter == 0)
         def _():
             parts[b, 0] = jnp.ones((ROWS, Y), F32)
-            for i in (1, 2, 3):
-                parts[b, i] = jnp.zeros((ROWS, Y), F32)
-
-        @pl.when((k & 1) == 1)
-        def _():
-            wait_back(b)
-
-        @pl.when(jnp.logical_and((k & 1) == 1, k < 2 * DEPTH - 1))
-        def _():
-            wait_front(lax.rem(b + 1, DEPTH))
+            for p in (1, 2, 3):
+                parts[b, p] = jnp.zeros((ROWS, Y), F32)
+
+        pl.when(quarter == 2)(lambda: wait_back(b))
+        pl.when(jnp.logical_and(quarter == 3, i < DEPTH - 1))(lambda: wait_front(block(i + 1)))
 
         for h in range(2):
-            @pl.when(k + me >= 0)
+
+            @pl.when((m & 1) == h)
             def _(h=h):
-                n = 4 * k + 2 * h
                 use, fill = 2 * h, 2 - 2 * h
-                slopes_y(n + 2, fill)
-                for i in range(8):
-                    slopes_zx(n + 2 + i // 4, fill + i // 4, i % 4)
-                    march(n + i % 2, use + i % 2, i // 2)
-
-        @pl.when(jnp.logical_and((k & 1) == 1, k < 2 * DEPTH - 2))
+                slopes_y(2 * m + 2, fill)
+                for p in range(8):
+                    slopes_zx(2 * m + 2 + p // 4, fill + p // 4, p % 4)
+                    after = [slots[fill + (p - LAG) // 4][1].at[0, 2 * ((p - LAG) % 4)]] if p >= LAG else []
+                    if p in (5, 6):
+                        after.append(slots[fill + (p == ((5, 6))[1])][0].at[7])
+                    march(2 * m + p % 2, use + p % 2, p // 2, after)
+
+        @pl.when(jnp.logical_and(quarter == 3, i < DEPTH - 1))
         def _():
             send(b).start()
 
         return 0
 
-    lax.fori_loop(0, 2 * DEPTH, half_block, 0)
+    lax.fori_loop(0, 4 * DEPTH, turn, 0)
 
     got[me] = parts[me]
     for step in range(1, DEPTH):
@@ -303,9 +321,9 @@
         r_sum += through * got[i, 2]
         g_sum += through * got[i, 3]
         through = through * got[i, 0]
-    out_ref[0] = (w_sum + r_sum) * (0.5 * 0.7 / 25.0)
-    out_ref[1] = g_sum * (0.7 / 25.0)
-    out_ref[2] = (w_sum - r_sum) * (0.5 * 0.7 / 25.0)
+    out_ref[0] = (w_sum + r_sum) * (0.5 * SCALE)
+    out_ref[1] = g_sum * SCALE
+    out_ref[2] = (w_sum - r_sum) * (0.5 * SCALE)
     out_ref[3] = 1.0 - through
 
     for step in range(1, DEPTH):

time: 38.5 us -> 37.6 us (0.977)
  Pallas kernels: 37.7 us -> 36.8 us
    pallas_call x1, Pallas kernels: 37.7 us -> 36.8 us  [on_device(): pl.pallas_call(kernel, out_shape=jax.ShapeDtypeStruct((4, ROWS, Y), F32),...]
where the time goes in v5:
time: 37.6 us; the launch traced here: 37.5 us
  Pallas kernels  36.8 us (98%)
  local copies, waits for them, and re-layouts  0.66 us (2%)
    pallas_call x1, Pallas kernels, on_device(): pl.pallas_call(kernel, out_shape=jax.ShapeDtypeStruct((4, ROWS, Y), F32),...  36.8 us

profile of v5, /device:TPU:1, one launch (start us, length us, event | category | flops | bytes accessed | tf_op | source)
XLA Modules:
  0.0 37.5 jit_solution(8841327680521412377)
XLA Ops:
  0.0 36.8 %render.1 = f32[4,32,256]{2,1,0:T(8,128)S(1)} custom-call(bf16[64,256,256]{2,1,0:T(8,128)(2,1)} %x_ref.1), custom_call_target="tpu_custom_call" | custom-call | tf_op jit(solution)/shard_map/render/pallas_call | solution.py:345
  36.8 0.7 %copy.3 = f32[4,32,256]{2,1,0:T(8,128)} copy(f32[4,32,256]{2,1,0:T(8,128)S(1)} %render.1) | data formatting | bytes 262144

commit v6 on v5

--- a/solution.py
+++ b/solution.py
@@ -58,8 +58,8 @@
     left, right = iy > 0, iy < n_iy - 1
 
     def block(i, at=me):
-        swap = jnp.where(at == 7, 1, jnp.where(at == 6, 2, 0))
-        return lax.rem(at + 1 + jnp.where(i <= swap, swap - i, i), DEPTH)
+        swapped = jnp.where(jnp.logical_and(jnp.logical_or(at == 0, at == DEPTH - 1), i < 2), 1 - i, i)
+        return lax.rem(jnp.where((at & 1) == 1, at + 1 + swapped, at + 2 * DEPTH - 1 - swapped), DEPTH)
 
     def load(b):
         rows = pl.ds(pl.multiple_of(ROWS * b, ROWS), ROWS)

time: 37.6 us -> 35.2 us (0.936)
  Pallas kernels: 36.8 us -> 34.3 us
    pallas_call x1, Pallas kernels: 36.8 us -> 34.3 us  [on_device(): pl.pallas_call(kernel, out_shape=jax.ShapeDtypeStruct((4, ROWS, Y), F32),...]
where the time goes in v6:
time: 35.2 us; the launch traced here: 35 us
  Pallas kernels  34.3 us (97%)
  local copies, waits for them, and re-layouts  0.66 us (2%)
    pallas_call x1, Pallas kernels, on_device(): pl.pallas_call(kernel, out_shape=jax.ShapeDtypeStruct((4, ROWS, Y), F32),...  34.3 us

profile of v6, /device:TPU:1, one launch (start us, length us, event | category | flops | bytes accessed | tf_op | source)
XLA Modules:
  0.0 35.0 jit_solution(9633954146546335378)
XLA Ops:
  0.0 34.3 %render.1 = f32[4,32,256]{2,1,0:T(8,128)S(1)} custom-call(bf16[64,256,256]{2,1,0:T(8,128)(2,1)} %x_ref.1), custom_call_target="tpu_custom_call" | custom-call | tf_op jit(solution)/shard_map/render/pallas_call | solution.py:345
  34.3 0.7 %copy.3 = f32[4,32,256]{2,1,0:T(8,128)} copy(f32[4,32,256]{2,1,0:T(8,128)S(1)} %render.1) | data formatting | bytes 262144

commit v7 on v6

--- a/solution.py
+++ b/solution.py
@@ -29,7 +29,8 @@
 def fill_matrices(y_mat, zx_mat, pick, spread):
     k, y = (lax.broadcasted_iota(jnp.int32, (256, Y), i) for i in (0, 1))
     y_mat[:256] = tap(k - y).astype(BF16)
-    y_mat[256:] = tap(jnp.where(k < 128, (k & 1) - 2, Y + (k & 1)) - y).astype(BF16)
+    low = (k & 64) == ((k & 128) >> 1)
+    y_mat[256:] = tap(jnp.where(low, (k & 1) - 2, Y + (k & 1)) - y).astype(BF16)
     m, c = (lax.broadcasted_iota(jnp.int32, (2 * ROWS, 256), i) for i in (0, 1))
     layer, row = m >> 5, m & 31
     at = jnp.where(c < 64, c >> 5, jnp.where(c < 192, 1 + (c >> 6), (c >> 5) - 2))
@@ -142,6 +143,7 @@
             first = jnp.where(lane >> 1 == z, moved, first)
             last = jnp.where(lane >> 1 == (z + 63) & 63, moved, last)
         last = pltpu.roll(last, 2, axis=1)
+        first = pltpu.roll(first, 64, axis=1)
         at = pl.ds(pl.multiple_of(16 * half, 16), 16)
         pack[0, b, at] = first.astype(BF16)
         pack[1, b, at] = last.astype(BF16)
@@ -172,12 +174,14 @@
     def slopes_y(n, first):
         b, c = place(n)
         inner = pl.ds(pl.multiple_of(EDGE + ROWS * b, EDGE), ROWS)
-        sides = jnp.concatenate([halo[0, b], halo[1, b]], axis=1)
-        layer_of = (lax.broadcasted_iota(jnp.int32, (ROWS, 256), 1) & 127) >> 1
+        lanes = lax.broadcasted_iota(jnp.int32, (ROWS, 128), 1)
+        late = c >> 2
+        sides = jnp.where(lanes < 64, halo[late, b], halo[1 - late, b])
+        layer_of = ((lanes & 63) >> 1) + 32 * late
         outer = jnp.stack([jnp.where(layer_of == 8 * c + i, sides, jnp.zeros_like(sides)) for i in range(16)])
         tiles = cells[pl.ds(2 + 8 * c, 16), inner].reshape(16 * ROWS, Y)
         gy = jnp.dot(tiles, y_mat[:Y], preferred_element_type=F32)
-        gy += jnp.dot(outer.reshape(16 * ROWS, 256), y_mat[Y:], preferred_element_type=F32)
+        gy += jnp.dot(outer.reshape(16 * ROWS, 128), y_mat[pl.ds(pl.multiple_of(Y + 128 * late, 128), 128)], preferred_element_type=F32)
         gy = gy.reshape(2, 8, ROWS, Y)
         slots[first][0][...] = gy[0]
         slots[first + 1][0][...] = gy[1]
@@ -295,7 +299,7 @@
                     slopes_zx(2 * m + 2 + p // 4, fill + p // 4, p % 4)
                     after = [slots[fill + (p - LAG) // 4][1].at[0, 2 * ((p - LAG) % 4)]] if p >= LAG else []
                     if p in (5, 6):
-                        after.append(slots[fill + (p == ((5, 6))[1])][0].at[7])
+                        after.append(slots[fill + (p == 6)][0].at[7])
                     march(2 * m + p % 2, use + p % 2, p // 2, after)
 
         @pl.when(jnp.logical_and(quarter == 3, i < DEPTH - 1))

time: 35.2 us -> 35.1 us (level)
  no operation moved by 1% of the time
where the time goes in v7:
time: 35.1 us; the launch traced here: 34.9 us
  Pallas kernels  34.2 us (97%)
  local copies, waits for them, and re-layouts  0.66 us (2%)
    pallas_call x1, Pallas kernels, on_device(): pl.pallas_call(kernel, out_shape=jax.ShapeDtypeStruct((4, ROWS, Y), F32),...  34.2 us

profile of v7, /device:TPU:1, one launch (start us, length us, event | category | flops | bytes accessed | tf_op | source)
XLA Modules:
  0.0 34.9 jit_solution(5073020731908802704)
XLA Ops:
  0.0 34.2 %render.1 = f32[4,32,256]{2,1,0:T(8,128)S(1)} custom-call(bf16[64,256,256]{2,1,0:T(8,128)(2,1)} %x_ref.1), custom_call_target="tpu_custom_call" | custom-call | tf_op jit(solution)/shard_map/render/pallas_call | solution.py:349
  34.3 0.7 %copy.3 = f32[4,32,256]{2,1,0:T(8,128)} copy(f32[4,32,256]{2,1,0:T(8,128)S(1)} %render.1) | data formatting | bytes 262144

commit v8 on v7

--- a/solution.py
+++ b/solution.py
@@ -13,7 +13,7 @@
 ROWS = X // DEPTH
 EDGE = 16
 NZ = 512
-LAG = 3
+LAG = 2
 EXP2_2D = float(2.0 * np.log2(np.e))
 EXP2_K = float(-0.1 * np.log2(np.e) / NZ)
 EXP2_SQ = float(-np.log2(np.e))

time: 35.1 us -> 34.7 us (0.989)
  Pallas kernels: 34.2 us -> 33.8 us
    pallas_call x1, Pallas kernels: 34.2 us -> 33.8 us  [on_device(): pl.pallas_call(kernel, out_shape=jax.ShapeDtypeStruct((4, ROWS, Y), F32),...]
where the time goes in v8:
time: 34.7 us; the launch traced here: 34.5 us
  Pallas kernels  33.8 us (97%)
  local copies, waits for them, and re-layouts  0.66 us (2%)
    pallas_call x1, Pallas kernels, on_device(): pl.pallas_call(kernel, out_shape=jax.ShapeDtypeStruct((4, ROWS, Y), F32),...  33.8 us

profile of v8, /device:TPU:1, one launch (start us, length us, event | category | flops | bytes accessed | tf_op | source)
XLA Modules:
  0.0 34.5 jit_solution(9941798946803543031)
XLA Ops:
  0.0 33.8 %render.1 = f32[4,32,256]{2,1,0:T(8,128)S(1)} custom-call(bf16[64,256,256]{2,1,0:T(8,128)(2,1)} %x_ref.1), custom_call_target="tpu_custom_call" | custom-call | tf_op jit(solution)/shard_map/render/pallas_call | solution.py:349
  33.8 0.7 %copy.3 = f32[4,32,256]{2,1,0:T(8,128)} copy(f32[4,32,256]{2,1,0:T(8,128)S(1)} %render.1) | data formatting | bytes 262144
